TPU v7x, 128 devices: a whole 4x4x4 slice. The times are simulated.
128 devices in a mesh: row: 16 (over x, z), col: 8 (over y, core).
Axes of the slice: x: 4, y: 4, z: 4, core: 2. Of those that a mesh axis runs over, the one named last changes fastest.
Arguments:
- positions: float32 [3, 32768], P(None, ('row', 'col')), may hold values from 0 to 4
- primal: bfloat16 [32768, 32], P(('row', 'col')), may hold values from -0.59765625 to 0.59765625
- adjoint: bfloat16 [32768, 32], P(('row', 'col')), may hold values from -0.59765625 to 0.59765625
- support: int32 [4, 32768], P(None, ('row', 'col')), may hold values from 0 to 2047
- basis: float32 [4, 32768], P(None, ('row', 'col')), may hold values from 0.1 to 1
Outputs:
- cp_gradient: float32 [3, 2048], P(None, ('row', 'col'))
All inputs are finite; a program needn't handle non-finite values.
Results may differ from a plain program's by a relative error of at most 0.0011.
Values may be sent and summed in bfloat16 or wider, within the bound.
A program may use at most 64 MiB of HBM per device.

v0:
```python
import jax
import jax.numpy as jnp
from jax import lax
from jax.sharding import PartitionSpec as P

CP = 2048


core_sq = 0.01


def pair_terms(xt, xs, weights):
    dist = core_sq + (xt[0][:, None] - xs[0][None, :]) ** 2
    dist = dist + (xt[1][:, None] - xs[1][None, :]) ** 2
    dist = dist + (xt[2][:, None] - xs[2][None, :]) ** 2
    inverse = lax.rsqrt(dist)
    paired = weights * inverse * inverse * inverse
    aug_t = jnp.concatenate([xt, jnp.ones((1, xt.shape[1]), xt.dtype)], 0)
    aug_s = jnp.concatenate([xs, jnp.ones((1, xs.shape[1]), xs.dtype)], 0)
    upper = jnp.dot(aug_t, paired, precision=lax.Precision.HIGHEST)
    lower = lax.dot_general(
        aug_s, paired, (((1,), (1,)), ((), ())), precision=lax.Precision.HIGHEST
    )
    source_part = upper[:3] - xs * upper[3:4]
    target_part = lower[:3] - xt * lower[3:4]
    return (source_part, target_part)


def to_points(total, grad, sup, bas):
    for k in range(sup.shape[0]):
        total = total.at[:, sup[k]].add(bas[k][None, :] * grad)
    return total


def shards(positions, primal, adjoint, support, basis):
    tpos, tbas = (
        lax.all_gather(positions, "col", axis=1, tiled=True),
        lax.all_gather(basis, "col", axis=1, tiled=True),
    )
    tadj = lax.all_gather(adjoint, "col", axis=0, tiled=True)
    tsup = lax.all_gather(support, "col", axis=1, tiled=True)
    apos, abas = (
        lax.all_gather(positions, ("row", "col"), axis=1, tiled=True),
        lax.all_gather(basis, ("row", "col"), axis=1, tiled=True),
    )
    aprim = lax.all_gather(primal, ("row", "col"), axis=0, tiled=True)
    asup = lax.all_gather(support, ("row", "col"), axis=1, tiled=True)
    width = apos.shape[1] // lax.axis_size("col")
    first = lax.axis_index("col") * width
    spos = lax.dynamic_slice_in_dim(apos, first, width, 1)
    sprim = lax.dynamic_slice_in_dim(aprim, first, width, 0)
    ssup = lax.dynamic_slice_in_dim(asup, first, width, 1)
    sbas = lax.dynamic_slice_in_dim(abas, first, width, 1)
    rows_here = tpos.shape[1]
    blk = min(512, rows_here)

    def block(k, carry):
        src, tgt = carry
        start = (k * blk).astype(jnp.int32)
        xt = lax.dynamic_slice_in_dim(tpos, start, blk, 1)
        lt = lax.dynamic_slice_in_dim(tadj, start, blk, 0)
        weights = lax.dot_general(
            lt, sprim, (((1,), (1,)), ((), ())), preferred_element_type=jnp.float32
        )
        part_src, part_tgt = pair_terms(xt, spos, weights)
        tgt = lax.dynamic_update_slice_in_dim(tgt, part_tgt, start, 1)
        return (src + part_src, tgt)

    src_zero = jnp.zeros(spos.shape, jnp.float32)
    tgt_zero = jnp.zeros(tpos.shape, jnp.float32)
    src, tgt = lax.fori_loop(0, rows_here // blk, block, (src_zero, tgt_zero))
    total = jnp.zeros((3, CP), jnp.float32)
    total = to_points(total, src, ssup, sbas)
    total = to_points(total, tgt, tsup, tbas)
    return lax.psum_scatter(total, ("row", "col"), scatter_dimension=1, tiled=True)


def solution(mesh):
    in_specs = (
        P(None, ("row", "col")),
        P(("row", "col"), None),
        P(("row", "col"), None),
        P(None, ("row", "col")),
        P(None, ("row", "col")),
    )
    out_specs = P(None, ("row", "col"))
    return jax.shard_map(shards, mesh=mesh, in_specs=in_specs, out_specs=out_specs, check_vma=False)
```

profile of v0, /device:TPU:1, one launch (start us, length us, event | category | flops | bytes accessed | tf_op | source)
XLA Modules:
  0.0 1020.8 jit_solution(6093477024321833386)
XLA Ops:
  8.9 14.8 %all_gather.26 = f32[3,2048]{1,0:T(4,128)S(1)} all-gather(f32[3,256]{1,0:T(4,128)} %param.7), channel_id=1, replica_groups=mesh['row'=16,'col'=8] {'col'}, dimensions={1}, use_global_device_ids=true | all-gather | bytes 27648 | tf_op jit(solution)/shard_map/all_gather | solution.py:37
  23.7 13.0 %all_gather.31 = f32[4,2048]{1,0:T(4,128)S(1)} all-gather(f32[4,256]{1,0:T(4,128)} %param.11), channel_id=1, replica_groups=mesh['row'=16,'col'=8] {'col'}, dimensions={1}, use_global_device_ids=true | all-gather | bytes 36864 | tf_op jit(solution)/shard_map/all_gather | solution.py:38
  36.6 12.9 %all_gather.30 = s32[4,2048]{1,0:T(4,128)S(1)} all-gather(s32[4,256]{1,0:T(4,128)} %param.10), channel_id=1, replica_groups=mesh['row'=16,'col'=8] {'col'}, dimensions={1}, use_global_device_ids=true | all-gather | bytes 36864 | tf_op jit(solution)/shard_map/all_gather | solution.py:41
  49.6 13.1 %all_gather.27 = bf16[2048,32]{1,0:T(8,128)(2,1)S(1)} all-gather(bf16[256,32]{1,0:T(8,128)(2,1)S(1)} %copy.18), channel_id=1, replica_groups=mesh['row'=16,'col'=8] {'col'}, dimensions={0}, use_global_device_ids=true | all-gather | bytes 147456 | tf_op jit(solution)/shard_map/all_gather | solution.py:40
  62.7 37.4 %all_gather.29 = f32[3,32768]{1,0:T(4,128)S(1)} all-gather(f32[3,256]{1,0:T(4,128)} %param.7), channel_id=1, replica_groups=mesh['row'=16,'col'=8] {'row','col'}, dimensions={1}, use_global_device_ids=true | all-gather | bytes 396288 | tf_op jit(solution)/shard_map/all_gather | solution.py:43
  100.1 33.8 %all_gather.25 = f32[4,32768]{1,0:T(4,128)S(1)} all-gather(f32[4,256]{1,0:T(4,128)} %param.11), channel_id=1, replica_groups=mesh['row'=16,'col'=8] {'row','col'}, dimensions={1}, use_global_device_ids=true | all-gather | bytes 528384 | tf_op jit(solution)/shard_map/all_gather | solution.py:44
  133.9 33.8 %all_gather.24 = s32[4,32768]{1,0:T(4,128)S(1)} all-gather(s32[4,256]{1,0:T(4,128)} %param.10), channel_id=1, replica_groups=mesh['row'=16,'col'=8] {'row','col'}, dimensions={1}, use_global_device_ids=true | all-gather | bytes 528384 | tf_op jit(solution)/shard_map/all_gather | solution.py:47
  169.5 60.5 %while.16 = (s32[]{:T(128)}, f32[3,4096]{1,0:T(4,128)S(1)}, f32[3,2048]{1,0:T(4,128)S(1)}, f32[3,2048]{1,0:T(4,128)S(1)}, bf16[2048,32]{1,0:T(8,128)(2,1)S(1)}, ...) while((s32[]{:T(128)}, f32[3,4096]{1,0:T(4,128)S(1)}, ...), condition=%wide.region_1.0_spmd.clone, body=%wide.region_0.0_spmd.clone.sunk | while | flops 360762368 | bytes 26925280 | solution.py:71
  173.6 6.9 fusion.36
  180.6 4.0 fusion.38
  188.7 6.9 fusion.36
  195.6 4.0 fusion.38
  203.7 6.9 fusion.36
  210.7 4.0 fusion.38
  218.8 6.9 fusion.36
  242.3 22.9 %scatter_custom_fusion = f32[3,2048]{0,1:T(8,128)S(1)} fusion(s32[4096]{0:T(1024)S(1)} %bitcast.120, f32[4096,3]{1,0:T(8,128)} %copy.21, f32[]{:T(128)} %constant.53.clone.1), kind=kCustom, calls=%fused_computation.23 | custom fusion | flops 12288 | bytes 25088 | tf_op jit(solution)/shard_map/scatter-add | solution.py:31
  265.2 23.1 %scatter_fusion = f32[3,2048]{0,1:T(8,128)S(1)} fusion(f32[3,2048]{0,1:T(8,128)S(1)} %scatter_custom_fusion, s32[4096]{0:T(1024)S(1)} %bitcast.104, f32[4096,3]{1,0:T(8,128)} %copy.22), kind=kCustom, calls=%fused_computation.1 | custom fusion | flops 12288 | bytes 163840 | tf_op jit(solution)/shard_map/scatter-add | solution.py:31
  288.2 23.1 %scatter_fusion.1 = f32[3,2048]{0,1:T(8,128)S(1)} fusion(f32[3,2048]{0,1:T(8,128)S(1)} %scatter_fusion, s32[4096]{0:T(1024)S(1)} %bitcast.103, f32[4096,3]{1,0:T(8,128)} %copy.23), kind=kCustom, calls=%fused_computation.2 | custom fusion | flops 12288 | bytes 163840 | tf_op jit(solution)/shard_map/scatter-add | solution.py:31
  311.3 22.8 %scatter_fusion.2 = f32[3,2048]{0,1:T(8,128)S(1)} fusion(f32[3,2048]{0,1:T(8,128)S(1)} %scatter_fusion.1, s32[4096]{0:T(1024)S(1)} %bitcast.102, f32[4096,3]{1,0:T(8,128)S(1)} %copy.24), kind=kCustom, calls=%fused_computation.3 | custom fusion | flops 12288 | bytes 163840 | tf_op jit(solution)/shard_map/scatter-add | solution.py:31
  334.1 12.2 %scatter_fusion.3 = f32[3,2048]{0,1:T(8,128)S(1)} fusion(f32[3,2048]{0,1:T(8,128)S(1)} %scatter_fusion.2, s32[2048]{0:T(1024)S(1)} %bitcast.115, f32[2048,3]{1,0:T(8,128)} %copy.25), kind=kCustom, calls=%fused_computation.4 | custom fusion | flops 6144 | bytes 81920 | tf_op jit(solution)/shard_map/scatter-add | solution.py:31
  346.3 12.5 %scatter_fusion.4 = f32[3,2048]{0,1:T(8,128)S(1)} fusion(f32[3,2048]{0,1:T(8,128)S(1)} %scatter_fusion.3, s32[2048]{0:T(1024)S(1)} %bitcast.114, f32[2048,3]{1,0:T(8,128)} %copy.26), kind=kCustom, calls=%fused_computation.5 | custom fusion | flops 6144 | bytes 81920 | tf_op jit(solution)/shard_map/scatter-add | solution.py:31
  358.8 12.2 %scatter_fusion.5 = f32[3,2048]{0,1:T(8,128)S(1)} fusion(f32[3,2048]{0,1:T(8,128)S(1)} %scatter_fusion.4, s32[2048]{0:T(1024)S(1)} %bitcast.113, f32[2048,3]{1,0:T(8,128)} %copy.27), kind=kCustom, calls=%fused_computation.6 | custom fusion | flops 6144 | bytes 81920 | tf_op jit(solution)/shard_map/scatter-add | solution.py:31
  371.1 12.2 %scatter_fusion.6 = f32[3,2048]{0,1:T(8,128)S(1)} fusion(f32[3,2048]{0,1:T(8,128)S(1)} %scatter_fusion.5, s32[2048]{0:T(1024)S(1)} %bitcast.112, f32[2048,3]{1,0:T(8,128)} %copy.28), kind=kCustom, calls=%fused_computation.7 | custom fusion | flops 6144 | bytes 81920 | tf_op jit(solution)/shard_map/scatter-add | solution.py:31
  384.3 627.8 %reduce-scatter.2.cloned.1.call-done = f32[3,16]{0,1:T(8,128)} async-done(((f32[3,2048]{0,1:T(8,128)}), f32[3,16]{0,1:T(8,128)}) %reduce-scatter.2.cloned.1.call-update) | async-done | bytes 208 | tf_op jit(solution)/shard_map/reduce_scatter | solution.py:75
  (57 shorter events, 38.8 us)
Async XLA Ops:
  6.5 161.7 %all-gather.2.cloned.1.call-start = ((), (), s32[]{:S(2)}) async-start(), calls=%async_computation.1 | async-start | bytes 8454144 | tf_op jit(solution)/shard_map/all_gather | solution.py:46
  8.0 1004.1 %reduce-scatter.2.cloned.1.call-start = ((), (), s32[]{:S(2)}) async-start(), calls=%async_computation.2 | async-start | bytes 1056768 | tf_op jit(solution)/shard_map/reduce_scatter | solution.py:75
  383.3 1.0 copy-start
Sparse Core Ops, SparseCore 0:
  10.3 73.9 all-gather.1
  384.4 627.6 reduce-scatter.1
where the time goes:
time: 1030 us; the launch traced here: 1020 us
  waiting for transfers between devices  628 us (61%)
  blocking collectives  159 us (15%)
  other arithmetic  142 us (14%)
  matrix products  59 us (6%)
  local copies, waits for them, and re-layouts  18.8 us (2%)
  between operations  14 us (1%)
    reduce_scatter x1, waiting for transfers between devices, shards(): lax.psum_scatter(total, ('row', 'col'), scatter_dimension=1, tiled=True)  628 us
    scatter-add x8, other arithmetic, to_points(): total = total.at[:, sup[k]].add(bas[k][None, :] * grad)  141 us
    all_gather x1, blocking collectives, shards(): lax.all_gather(positions, ('row', 'col'), axis=1, tiled=True)  37.4 us
    all_gather x1, blocking collectives, shards(): asup = lax.all_gather(support, ('row', 'col'), axis=1, tiled=True)  33.8 us
    all_gather x1, blocking collectives, shards(): lax.all_gather(basis, ('row', 'col'), axis=1, tiled=True)  33.8 us
    dot_general x4, matrix products, pair_terms(): lax.dot_general(aug_s, paired, (((1,), (1,)), ((), ())), precision=lax.Pr...  27.7 us
  transfers between devices with their start and end apart: 2, of which 1 were waited for; matrix products, arithmetic and copies ran while one was open for 0% of the time, Pallas kernels for 0%

commit v1 on v0

v1 whole, which is shorter than its diff:
```python
import numpy as np
import jax
import jax.numpy as jnp
from jax import lax
from jax.experimental import pallas as pl
from jax.experimental.pallas import tpu as pltpu
from jax.sharding import PartitionSpec as P

f32, bf16 = jnp.float32, jnp.bfloat16
MESH = pl.DeviceIdType.MESH
NT = (((1,), (1,)), ((), ()))
TN = (((0,), (0,)), ((), ()))

STR, CP, CORE_SQ, SHIFT = 32, 2048, 0.01, 2.0
PB = 256
NCOL, NROW, SIDE = 8, 16, 4
FULL = ((1, 0), (0, 1), (1, 1), (3, 1), (3, 2), (2, 3))
HALF = ((2, 0), (0, 2), (2, 2))
OFFS = FULL + HALF
ROWS = 96
CHUNK = 32


def selectors():
    left = np.zeros((80, 512), np.float32)
    for s in range(STR):
        left[STR + s, s] = 1.0
        left[s, STR + s] = 1.0
    h, m, l, n, one = 64, 67, 70, 73, 76
    for part, rows in enumerate((h, m, l)):
        base = 64 + 16 * part
        for c in range(3):
            for slot in (c, 3 + c, 6 + c):
                left[rows + c, base + slot] = -2.0
        left[n + part, base + 12] = 1.0
    for k in range(3):
        left[one, 64 + 9 + k] = 1.0
    for c in range(3):
        for rows in (h, m, l):
            left[rows + c, 128 + 128 * c : 256 + 128 * c] = 1.0
    return left


def split3(x):
    h = x.astype(bf16)
    rest = x - h.astype(f32)
    m = rest.astype(bf16)
    return h, m, (rest - m.astype(f32)).astype(bf16)


def kernel(
    pos_ref, prim_ref, adj_ref, sup_ref, bas_ref, sel_ref, eye_ref, out_ref,
    ta, tb, aw, ad, xa, acc_a, acc_b, grad_a, s1, r1, s2, r2,
    send_a, recv_a, send_b, recv_b, send_1, recv_1, send_2, recv_2,
):
    row, col = lax.axis_index("row"), lax.axis_index("col")
    rx, rz = row // SIDE, row % SIDE

    def at_row(off):
        return ((rx + off[0]) % SIDE) * SIDE + (rz + off[1]) % SIDE

    def at_col(d):
        return (col + d) % NCOL

    barrier = pltpu.get_barrier_semaphore()
    for d in range(1, NCOL):
        pl.semaphore_signal(barrier, inc=1, device_id=(row, at_col(d)), device_id_type=MESH)
    for k in range(1, NROW):
        other = at_row((k // SIDE, k % SIDE))
        pl.semaphore_signal(barrier, inc=1, device_id=(other, col), device_id_type=MESH)

    eye = eye_ref[...]
    ta[0, 0:32] = lax.dot_general(eye, adj_ref[...], NT, preferred_element_type=f32).astype(bf16)
    ta[0, 32:64] = lax.dot_general(eye, prim_ref[...], NT, preferred_element_type=f32).astype(bf16)
    u = pos_ref[...] - SHIFT
    n = jnp.sum(u * u, axis=0, keepdims=True) + 0.5 * CORE_SQ
    uh, um, ul = split3(u)
    nh, nm, nl = split3(n)
    feats = [p.astype(f32) for p in (uh, um, ul, nh, nm, nl)]
    feats.append(jnp.ones((1, PB), f32))
    feats.append(jnp.zeros((3, PB), f32))
    ta[0, 64:80] = jnp.concatenate(feats, axis=0).astype(bf16)
    sup = sup_ref[...]
    bas = bas_ref[...]
    bh = bas.astype(bf16).astype(f32)
    bm = bas - bh
    ta[0, 80:96] = jnp.concatenate(
        [(sup // 128).astype(f32), (sup % 128).astype(f32), bh, bm], axis=0
    ).astype(bf16)

    pl.semaphore_wait(barrier, NCOL - 1 + NROW - 1)

    def copy_a(d):
        return pltpu.make_async_remote_copy(
            src_ref=ta.at[0], dst_ref=ta.at[d], send_sem=send_a.at[d - 1], recv_sem=recv_a.at[d - 1],
            device_id=(row, at_col(-d)), device_id_type=MESH,
        )

    def copy_b(k):
        off = OFFS[k]
        return pltpu.make_async_remote_copy(
            src_ref=ta.at[0], dst_ref=tb.at[k], send_sem=send_b.at[k], recv_sem=recv_b.at[k],
            device_id=(at_row((-off[0], -off[1])), col), device_id_type=MESH,
        )

    for d in range(1, 5):
        copy_a(d).start()
    for d in range(5, NCOL):
        copy_a(d).start()
    for k in range(len(OFFS)):
        copy_b(k).start()

    acc_a[...] = jnp.zeros_like(acc_a)

    def prepare(d):
        left = lax.dot_general(ta[d, 0:80], sel_ref[...], TN, preferred_element_type=f32)
        aw[d] = left[:, 0:64].astype(bf16)
        ad[d] = left[:, 64:112].astype(bf16)
        for c in range(3):
            xa[d, c] = left[:, 128 * (c + 1) : 128 * (c + 2)]

    def pairs(right, slots, store, half=()):
        parts = right[64:80]
        rd = jnp.concatenate([parts, parts, parts], axis=0)
        accs = [None] * 4
        for i, slot in enumerate(slots):
            rw = right[0:64]
            if i in half:
                rw = rw * jnp.asarray(0.5, bf16)
            w = jnp.dot(aw[slot], rw, preferred_element_type=f32)
            d = jnp.dot(ad[slot], rd, preferred_element_type=f32)
            his, los = [], []
            for q in range(PB // CHUNK):
                rs = slice(q * CHUNK, (q + 1) * CHUNK)
                inv = lax.rsqrt(d[rs])
                s = w[rs] * inv * (inv * inv)
                for c in range(4):
                    if c < 3:
                        x = xa[slot, c, rs]
                        t = s * jnp.concatenate([x, x], axis=1)
                    else:
                        t = s
                    t = jnp.sum(t.reshape(CHUNK // 8, 8, PB), axis=0)
                    accs[c] = t if accs[c] is None else accs[c] + t
                hi = s.astype(bf16)
                his.append(hi)
                los.append((s - hi.astype(f32)).astype(bf16))
            hi, lo = jnp.concatenate(his, axis=0), jnp.concatenate(los, axis=0)
            acc_a[slot] += lax.dot_general(parts, hi, NT, preferred_element_type=f32) + lax.dot_general(
                parts, lo, NT, preferred_element_type=f32
            )
        for c in range(4):
            acc_b[store, c] = accs[c]

    prepare(0)
    for d in range(1, 5):
        copy_a(d).wait_recv()
        prepare(d)
    pairs(ta.at[0], range(5), len(OFFS), half=(0, 4))
    for d in range(5, NCOL):
        copy_a(d).wait_recv()
        prepare(d)

    def full(k, _):
        pltpu.make_async_remote_copy(
            src_ref=ta.at[0], dst_ref=tb.at[k], send_sem=send_b.at[k], recv_sem=recv_b.at[k],
            device_id=(row, at_col(1)), device_id_type=MESH,
        ).wait_recv()
        pairs(tb.at[k], range(NCOL), k)
        return 0

    lax.fori_loop(0, len(FULL), full, 0)
    for k in range(len(FULL), len(OFFS)):
        copy_b(k).wait_recv()
        later = (at_row(OFFS[k]) < row).astype(jnp.int32)
        pairs(tb.at[k], [later + i for i in range(4)], k)

    def coords(bundle):
        p = bundle[64:80].astype(f32)
        return p[0:3] + p[3:6] + p[6:9]

    def from_b(k, bundle):
        sums = [jnp.sum(acc_b[k, c], axis=0, keepdims=True) for c in range(4)]
        return jnp.concatenate(sums[:3], axis=0) - coords(bundle) * sums[3]

    def from_a(d):
        t = acc_a[d]
        return t[0:3] + t[3:6] + t[6:9] - coords(ta.at[d]) * t[12:13]

    rows16 = lax.broadcasted_iota(jnp.int32, (16, PB), 0).astype(f32)
    rows128 = lax.broadcasted_iota(jnp.int32, (128, PB), 0).astype(f32)

    def scatter(total, grad, bundle):
        data = bundle[80:96].astype(f32)
        for k in range(4):
            val = grad * (data[8 + k : 9 + k] + data[12 + k : 13 + k])
            here = rows16 == data[k : k + 1]
            left = jnp.concatenate([jnp.where(here, val[c : c + 1], 0.0) for c in range(3)], axis=0)
            hi = left.astype(bf16)
            lo = (left - hi.astype(f32)).astype(bf16)
            hot = jnp.where(rows128 == data[4 + k : 5 + k], 1.0, 0.0).astype(bf16)
            total = total + lax.dot_general(hi, hot, NT, preferred_element_type=f32)
            total = total + lax.dot_general(lo, hot, NT, preferred_element_type=f32)
        return total

    total = jnp.zeros((48, 128), f32)
    total = scatter(total, from_a(0) + from_b(len(OFFS), ta.at[0]), ta.at[0])
    total = lax.fori_loop(1, NCOL, lambda d, t: scatter(t, from_a(d), ta.at[d]), total)
    total = lax.fori_loop(0, len(OFFS), lambda k, t: scatter(t, from_b(k, tb.at[k]), tb.at[k]), total)

    zeros = jnp.zeros((5, 128), f32)
    for q in range(NROW):
        s1[q] = jnp.concatenate([total[q : q + 1], total[16 + q : 17 + q], total[32 + q : 33 + q], zeros], axis=0)

    def copy_1(k):
        other = at_row((k // SIDE, k % SIDE))
        return pltpu.make_async_remote_copy(
            src_ref=s1.at[other], dst_ref=r1.at[k - 1], send_sem=send_1.at[k - 1], recv_sem=recv_1.at[k - 1],
            device_id=(other, col), device_id_type=MESH,
        )

    def copy_2(d):
        return pltpu.make_async_remote_copy(
            src_ref=s2, dst_ref=r2.at[d - 1], send_sem=send_2.at[d - 1], recv_sem=recv_2.at[d - 1],
            device_id=(row, at_col(d)), device_id_type=MESH,
        )

    for k in range(1, NROW):
        copy_1(k).start()
    mine = s1[row]
    for k in range(1, NROW):
        copy_1(k).wait_recv()
        mine = mine + r1[k - 1]
    s2[...] = mine
    for d in range(1, NCOL):
        copy_2(d).start()
    for d in range(1, NCOL):
        copy_2(d).wait_recv()
        mine = mine + r2[d - 1]
    mine = pltpu.roll(mine, (128 - 16 * col) % 128, 1)
    out_ref[...] = mine[0:3, 0:16]

    for d in range(1, NCOL):
        copy_a(d).wait_send()
        copy_2(d).wait_send()
    for k in range(len(OFFS)):
        copy_b(k).wait_send()
    for k in range(1, NROW):
        copy_1(k).wait_send()


def shards(positions, primal, adjoint, support, basis):
    sel = jnp.asarray(selectors(), bf16)
    eye = jnp.asarray(np.eye(STR, dtype=np.float32), bf16)
    vmem = pl.BlockSpec(memory_space=pltpu.VMEM)
    dma = pltpu.SemaphoreType.DMA
    nb = len(OFFS)
    return pl.pallas_call(
        kernel,
        out_shape=jax.ShapeDtypeStruct((3, 16), f32),
        in_specs=[vmem] * 7,
        out_specs=vmem,
        scratch_shapes=[
            pltpu.VMEM((NCOL, ROWS, PB), bf16),
            pltpu.VMEM((nb, ROWS, PB), bf16),
            pltpu.VMEM((NCOL, PB, 64), bf16),
            pltpu.VMEM((NCOL, PB, 48), bf16),
            pltpu.VMEM((NCOL, 3, PB, 128), f32),
            pltpu.VMEM((NCOL, 16, PB), f32),
            pltpu.VMEM((nb + 1, 4, 8, PB), f32),
            pltpu.VMEM((8, 128), f32),
            pltpu.VMEM((NROW, 8, 128), f32),
            pltpu.VMEM((NROW - 1, 8, 128), f32),
            pltpu.VMEM((8, 128), f32),
            pltpu.VMEM((NCOL - 1, 8, 128), f32),
            dma((NCOL - 1,)), dma((NCOL - 1,)), dma((nb,)), dma((nb,)),
            dma((NROW - 1,)), dma((NROW - 1,)), dma((NCOL - 1,)), dma((NCOL - 1,)),
        ],
        compiler_params=pltpu.CompilerParams(
            collective_id=0, has_side_effects=True, vmem_limit_bytes=48 * 2**20
        ),
    )(positions, primal, adjoint, support, basis, sel, eye)


def solution(mesh):
    in_specs = (
        P(None, ("row", "col")),
        P(("row", "col"), None),
        P(("row", "col"), None),
        P(None, ("row", "col")),
        P(None, ("row", "col")),
    )
    out_specs = P(None, ("row", "col"))
    return jax.shard_map(shards, mesh=mesh, in_specs=in_specs, out_specs=out_specs, check_vma=False)
```

time: 1030 us -> 45.3 us (0.04)
  waiting for transfers between devices: 628 us -> 0 us
  blocking collectives: 159 us -> 0 us
  other arithmetic: 142 us -> 0 us
  matrix products: 59 us -> 0 us
  Pallas kernels: 0 us -> 42.7 us
  local copies, waits for them, and re-layouts: 18.8 us -> 2.33 us
  between operations: 14 us -> 0.08 us
    reduce_scatter x1 -> x0, waiting for transfers between devices: 628 us -> none  [shards(): lax.psum_scatter(total, ('row', 'col'), scatter_dimension=1, tiled=True)]
    all_gather x7 -> x0, blocking collectives: 159 us -> none  [the longest x1 37.4 us: shards(): lax.all_gather(positions, ('row', 'col'), axis=1, tiled=True)]
    scatter-add x8 -> x0, other arithmetic: 141 us -> none  [to_points(): total = total.at[:, sup[k]].add(bas[k][None, :] * grad)]
    dot_general x12 -> x0, matrix products: 59 us -> none  [the longest x4 27.7 us: pair_terms(): lax.dot_general(aug_s, paired, (((1,), (1,)), ((), ())), precision=lax.Pr...]
    pallas_call x0 -> x1, Pallas kernels: none -> 42.7 us  [shards(): pl.pallas_call(kernel, out_shape=jax.ShapeDtypeStruct((3, 16), f32), in_s...]
    mul x8 -> x0, local copies, waits for them, and re-layouts: 12.1 us -> none  [to_points(): total = total.at[:, sup[k]].add(bas[k][None, :] * grad)]
  transfers between devices with their start and end apart: 2 -> 0, of which waited for: 1 -> 0; matrix products, arithmetic and copies ran while one was open for 0% -> 0% of each run, Pallas kernels for 0% -> 0%
where the time goes in v1:
time: 45.3 us; the launch traced here: 45.2 us
  Pallas kernels  42.7 us (94%)
  local copies, waits for them, and re-layouts  2.33 us (5%)
    pallas_call x1, Pallas kernels, shards(): pl.pallas_call(kernel, out_shape=jax.ShapeDtypeStruct((3, 16), f32), in_s...  42.7 us
    unnamed x13, local copies, waits for them, and re-layouts  2.33 us

profile of v1, /device:TPU:1, one launch (start us, length us, event | category | flops | bytes accessed | tf_op | source)
XLA Modules:
  0.0 45.2 jit_solution(8863997851665684077)
XLA Ops:
  0.0 0.0 copy-start
  0.0 0.9 %copy.8.prim_ref = bf16[256,32]{1,0:T(8,128)(2,1)S(1)} copy(bf16[256,32]{0,1:T(8,128)(2,1)} %param.8) | data formatting | bytes 32768 | tf_op args[1]
  0.9 0.0 copy-start.1
  0.9 0.0 copy-start.2
  0.9 0.0 copy-start.3
  0.9 0.0 copy-start.4
  0.9 0.9 %copy.9.adj_ref = bf16[256,32]{1,0:T(8,128)(2,1)S(1)} copy(bf16[256,32]{0,1:T(8,128)(2,1)} %param.9) | data formatting | bytes 32768 | tf_op args[2]
  1.8 0.0 copy-done
  1.8 0.0 copy-done.1
  1.8 0.0 copy-done.2
  1.8 0.0 copy-done.3
  1.8 0.0 copy-done.4
  1.8 42.7 %shard_map.73 = f32[3,16]{1,0:T(4,128)S(1)} custom-call(f32[3,256]{1,0:T(4,128)S(1)} %copy-done.2, bf16[256,32]{1,0:T(8,128)(2,1)S(1)} %copy.8.prim_ref, bf16[256,32]{1,0:T(8,128)(2,1)S(1)} %copy.9.adj_ref, s32[4,256]{1,0:T(4,128)S(1)} %copy-done.3, f32[4,256]{1,0:T(4,128)S(1)} %copy-done.4, bf16[80,512]{1,0:T(8,128)(2,1)S(1)} %copy-done, ...), custom_call_target="tpu_custom_call" | custom-call | tf_op jit(solution)/shard_map/pallas_call | solution.py:258
  44.6 0.6 %copy.11 = f32[3,16]{1,0:T(4,128)} copy(f32[3,16]{1,0:T(4,128)S(1)} %shard_map.73) | data formatting | bytes 384
Async XLA Ops:
  0.0 1.8 %copy-start = (bf16[80,512]{1,0:T(8,128)(2,1)S(1)}, bf16[80,512]{1,0:T(8,128)(2,1)}, u32[]{:S(2)}) copy-start(bf16[80,512]{1,0:T(8,128)(2,1)} %constant.4.clone.sel_ref) | copy-start | bytes 245764
  0.9 0.9 %copy-start.1 = (bf16[32,32]{1,0:T(8,128)(2,1)S(1)}, bf16[32,32]{1,0:T(8,128)(2,1)}, u32[]{:S(2)}) copy-start(bf16[32,32]{1,0:T(8,128)(2,1)} %constant.5.clone.eye_ref) | copy-start | bytes 6148
  0.9 0.9 %copy-start.2 = (f32[3,256]{1,0:T(4,128)S(1)}, f32[3,256]{1,0:T(4,128)}, u32[]{:S(2)}) copy-start(f32[3,256]{1,0:T(4,128)} %pos_ref.1) | copy-start | bytes 9220
  0.9 0.9 %copy-start.3 = (s32[4,256]{1,0:T(4,128)S(1)}, s32[4,256]{1,0:T(4,128)}, u32[]{:S(2)}) copy-start(s32[4,256]{1,0:T(4,128)} %sup_ref.1) | copy-start | bytes 12292
  0.9 0.9 %copy-start.4 = (f32[4,256]{1,0:T(4,128)S(1)}, f32[4,256]{1,0:T(4,128)}, u32[]{:S(2)}) copy-start(f32[4,256]{1,0:T(4,128)} %bas_ref.1) | copy-start | bytes 12292

commit v2 on v1

v2 whole, which is shorter than its diff:
```python
import numpy as np
import jax
import jax.numpy as jnp
from jax import lax
from jax.experimental import pallas as pl
from jax.experimental.pallas import tpu as pltpu
from jax.sharding import PartitionSpec as P

f32, bf16 = jnp.float32, jnp.bfloat16
MESH = pl.DeviceIdType.MESH
NT = (((1,), (1,)), ((), ()))
TN = (((0,), (0,)), ((), ()))

STR, CP, CORE_SQ, SHIFT = 32, 2048, 0.01, 2.0
PB = 256
NCOL, NROW, SIDE = 8, 16, 4
FULL = ((1, 0), (0, 1), (1, 1), (3, 1), (3, 2), (2, 3))
HALF = ((2, 0), (0, 2), (2, 2))
OFFS = FULL + HALF
ROWS = 96
CHUNK = 32


def selectors():
    left = np.zeros((80, 512), np.float32)
    for s in range(STR):
        left[STR + s, s] = 1.0
        left[s, STR + s] = 1.0
    h, m, l, n, one = 64, 67, 70, 73, 76
    for part, rows in enumerate((h, m, l)):
        base = 64 + 16 * part
        for c in range(3):
            for slot in (c, 3 + c, 6 + c):
                left[rows + c, base + slot] = -2.0
        left[n + part, base + 12] = 1.0
    for k in range(3):
        left[one, 64 + 9 + k] = 1.0
    for c in range(3):
        for rows in (h, m, l):
            left[rows + c, 128 + 128 * c : 256 + 128 * c] = 1.0
    return left


def split3(x):
    h = x.astype(bf16)
    rest = x - h.astype(f32)
    m = rest.astype(bf16)
    return h, m, (rest - m.astype(f32)).astype(bf16)


def kernel(
    pos_hbm, prim_hbm, adj_hbm, sup_hbm, bas_hbm, sel_hbm, out_ref,
    pos_v, sup_v, bas_v, sel_v, ta, tb, aw, ad, xa, acc_a, acc_b, s1, r1, s2, r2,
    load, send_a, recv_a, send_b, recv_b, send_1, recv_1, send_2, recv_2,
):
    row, col = lax.axis_index("row"), lax.axis_index("col")
    rx, rz, cy, core = row // SIDE, row % SIDE, col // 2, col % 2

    def at_row(off):
        return ((rx + off[0]) % SIDE) * SIDE + (rz + off[1]) % SIDE

    def at_col(slot, sign=1):
        return ((cy + sign * (slot // 2)) % SIDE) * 2 + (core + slot) % 2

    barrier = pltpu.get_barrier_semaphore()
    for slot in range(1, NCOL):
        pl.semaphore_signal(barrier, inc=1, device_id=(row, at_col(slot)), device_id_type=MESH)
    for k in range(1, NROW):
        other = at_row((k // SIDE, k % SIDE))
        pl.semaphore_signal(barrier, inc=1, device_id=(other, col), device_id_type=MESH)

    loads = [
        pltpu.make_async_copy(src, dst, load.at[i])
        for i, (src, dst) in enumerate((
            (pos_hbm, pos_v), (sup_hbm, sup_v), (bas_hbm, bas_v), (sel_hbm, sel_v),
            (adj_hbm, ta.at[0, 0:32]), (prim_hbm, ta.at[0, 32:64]),
        ))
    ]
    for copy in loads:
        copy.start()
    acc_a[...] = jnp.zeros_like(acc_a)
    for copy in loads[:3]:
        copy.wait()
    u = pos_v[...] - SHIFT
    n = jnp.sum(u * u, axis=0, keepdims=True) + 0.5 * CORE_SQ
    uh, um, ul = split3(u)
    nh, nm, nl = split3(n)
    feats = [p.astype(f32) for p in (uh, um, ul, nh, nm, nl)]
    feats.append(jnp.ones((1, PB), f32))
    feats.append(jnp.zeros((3, PB), f32))
    sup = sup_v[...]
    bas = bas_v[...]
    bh = bas.astype(bf16).astype(f32)
    feats += [(sup // 16).astype(f32), (sup % 16).astype(f32), bh, bas - bh]
    ta[0, 64:96] = jnp.concatenate(feats, axis=0).astype(bf16)
    for copy in loads[3:]:
        copy.wait()

    pl.semaphore_wait(barrier, NCOL - 1 + NROW - 1)

    def copy_a(slot):
        src = 0 if slot % 2 == 0 or slot == 1 else slot - 1
        to = at_col(slot, -1) if src == 0 else at_col(1)
        return pltpu.make_async_remote_copy(
            src_ref=ta.at[src], dst_ref=ta.at[slot], send_sem=send_a.at[slot - 1], recv_sem=recv_a.at[slot - 1],
            device_id=(row, to), device_id_type=MESH,
        )

    def copy_b(k):
        off = OFFS[k]
        return pltpu.make_async_remote_copy(
            src_ref=ta.at[0], dst_ref=tb.at[k], send_sem=send_b.at[k], recv_sem=recv_b.at[k],
            device_id=(at_row((-off[0], -off[1])), col), device_id_type=MESH,
        )

    for slot in (1, 2, 6, 4):
        copy_a(slot).start()
    for k in (0, 1):
        copy_b(k).start()

    def prepare(slot):
        left = lax.dot_general(ta[slot, 0:80], sel_v[...], TN, preferred_element_type=f32)
        aw[slot] = left[:, 0:64].astype(bf16)
        ad[slot] = left[:, 64:112].astype(bf16)
        for c in range(3):
            xa[slot, c] = left[:, 128 * (c + 1) : 128 * (c + 2)]

    def pairs(right, slots, store, half=(), first=True):
        parts = right[64:80]
        rd = jnp.concatenate([parts, parts, parts], axis=0)
        accs = [None] * 4
        for i, slot in enumerate(slots):
            rw = right[0:64]
            if i in half:
                rw = rw * jnp.asarray(0.5, bf16)
            w = jnp.dot(aw[slot], rw, preferred_element_type=f32)
            d = jnp.dot(ad[slot], rd, preferred_element_type=f32)
            his, los = [], []
            for q in range(PB // CHUNK):
                rs = slice(q * CHUNK, (q + 1) * CHUNK)
                inv = lax.rsqrt(d[rs])
                s = w[rs] * inv * (inv * inv)
                for c in range(4):
                    if c < 3:
                        x = xa[slot, c, rs]
                        t = s * jnp.concatenate([x, x], axis=1)
                    else:
                        t = s
                    t = jnp.sum(t.reshape(CHUNK // 8, 8, PB), axis=0)
                    accs[c] = t if accs[c] is None else accs[c] + t
                hi = s.astype(bf16)
                his.append(hi)
                los.append((s - hi.astype(f32)).astype(bf16))
            hi, lo = jnp.concatenate(his, axis=0), jnp.concatenate(los, axis=0)
            acc_a[slot] += lax.dot_general(parts, hi, NT, preferred_element_type=f32) + lax.dot_general(
                parts, lo, NT, preferred_element_type=f32
            )
        for c in range(4):
            acc_b[store, c] = accs[c] if first else acc_b[store, c] + accs[c]

    nb = len(OFFS)
    own = ta.at[0]
    prepare(0)
    pairs(own, [0], nb, half=(0,))
    copy_a(1).wait_recv()
    prepare(1)
    pairs(own, [1], nb, half=(0,), first=False)
    for slot in (2, 6, 4):
        copy_a(slot).wait_recv()
        copy_a(slot + 1).start()
    for k in (2, 3, 4):
        copy_b(k).start()
    prepare(2)
    prepare(4)
    prepare(6)
    pairs(own, [2, 4], nb, half=(1,), first=False)
    for k in range(5, nb):
        copy_b(k).start()
    for slot in (3, 7, 5):
        copy_a(slot).wait_recv()
        prepare(slot)
    pairs(own, [3, 5], nb, half=(1,), first=False)

    def arrived(k):
        pltpu.make_async_remote_copy(
            src_ref=ta.at[0], dst_ref=tb.at[k], send_sem=send_b.at[k], recv_sem=recv_b.at[k],
            device_id=(row, at_col(1)), device_id_type=MESH,
        ).wait_recv()

    def full(k, _):
        arrived(k)
        pairs(tb.at[k], range(NCOL), k)
        return 0

    def halved(k, _):
        arrived(k)
        i = k - len(FULL)
        first = 2 * (at_row((2 * ((i + 1) % 2), 2 * ((i + 1) // 2))) < row).astype(jnp.int32)
        pairs(tb.at[k], [first + j for j in range(4)], k)
        return 0

    lax.fori_loop(0, len(FULL), full, 0)
    lax.fori_loop(len(FULL), nb, halved, 0)

    def coords(bundle):
        p = bundle[64:80].astype(f32)
        return p[0:3] + p[3:6] + p[6:9]

    def from_b(k, bundle):
        sums = [jnp.sum(acc_b[k, c], axis=0, keepdims=True) for c in range(4)]
        return jnp.concatenate(sums[:3], axis=0) - coords(bundle) * sums[3]

    def from_a(slot):
        t = acc_a[slot]
        return t[0:3] + t[3:6] + t[6:9] - coords(ta.at[slot]) * t[12:13]

    rows16 = lax.broadcasted_iota(jnp.int32, (16, PB), 0).astype(f32).astype(bf16)
    rows128 = lax.broadcasted_iota(jnp.int32, (128, PB), 0).astype(f32).astype(bf16)
    zero, unit = jnp.zeros((), bf16), jnp.ones((), bf16)

    def scatter(total, grad, bundle):
        data = bundle[80:96]
        basis = data[8:12].astype(f32) + data[12:16].astype(f32)
        lefts, rights = [], []
        for k in range(4):
            val = grad * basis[k : k + 1]
            hi = val.astype(bf16)
            lo = (val - hi.astype(f32)).astype(bf16)
            here = rows16 == data[4 + k : 5 + k]
            rights.append(
                jnp.concatenate([jnp.where(here, p[c : c + 1], zero) for p in (hi, lo) for c in range(3)], axis=0)
            )
            lefts.append(jnp.where(rows128 == data[k : k + 1], unit, zero))
        left, right = jnp.concatenate(lefts, axis=1), jnp.concatenate(rights, axis=1)
        return total + lax.dot_general(left, right, NT, preferred_element_type=f32)

    total = jnp.zeros((128, 96), f32)
    total = scatter(total, from_a(0) + from_b(nb, own), own)
    total = lax.fori_loop(1, NCOL, lambda d, t: scatter(t, from_a(d), ta.at[d]), total)
    total = lax.fori_loop(0, nb, lambda k, t: scatter(t, from_b(k, tb.at[k]), tb.at[k]), total)
    total = jnp.concatenate([total[:, 0:48] + total[:, 48:96], jnp.zeros((128, 80), f32)], axis=1)

    s1[...] = total.reshape(NROW, NCOL, 128)

    def copy_1(k):
        other = at_row((k // SIDE, k % SIDE))
        return pltpu.make_async_remote_copy(
            src_ref=s1.at[other], dst_ref=r1.at[k - 1], send_sem=send_1.at[k - 1], recv_sem=recv_1.at[k - 1],
            device_id=(other, col), device_id_type=MESH,
        )

    def copy_2(slot):
        return pltpu.make_async_remote_copy(
            src_ref=s2, dst_ref=r2.at[slot - 1], send_sem=send_2.at[slot - 1], recv_sem=recv_2.at[slot - 1],
            device_id=(row, at_col(slot)), device_id_type=MESH,
        )

    for k in range(1, NROW):
        copy_1(k).start()
    mine = s1[row]
    for k in range(1, NROW):
        copy_1(k).wait_recv()
        mine = mine + r1[k - 1]
    s2[...] = mine
    for slot in range(1, NCOL):
        copy_2(slot).start()
    for slot in range(1, NCOL):
        copy_2(slot).wait_recv()
        mine = mine + r2[slot - 1]
    here = lax.broadcasted_iota(jnp.int32, (NCOL, 128), 0) == col
    line = jnp.sum(jnp.where(here, mine, 0.0), axis=0, keepdims=True)
    out_ref[...] = jnp.concatenate([line[:, 16 * c : 16 * (c + 1)] for c in range(3)], axis=0)

    for slot in range(1, NCOL):
        copy_a(slot).wait_send()
        copy_2(slot).wait_send()
    for k in range(nb):
        copy_b(k).wait_send()
    for k in range(1, NROW):
        copy_1(k).wait_send()


def shards(positions, primal, adjoint, support, basis):
    sel = jnp.asarray(selectors(), bf16)
    vmem = pl.BlockSpec(memory_space=pltpu.VMEM)
    hbm = pl.BlockSpec(memory_space=pltpu.HBM)
    dma = pltpu.SemaphoreType.DMA
    nb = len(OFFS)
    return pl.pallas_call(
        kernel,
        out_shape=jax.ShapeDtypeStruct((3, 16), f32),
        in_specs=[hbm] * 6,
        out_specs=vmem,
        scratch_shapes=[
            pltpu.VMEM((3, PB), f32),
            pltpu.VMEM((4, PB), jnp.int32),
            pltpu.VMEM((4, PB), f32),
            pltpu.VMEM((80, 512), bf16),
            pltpu.VMEM((NCOL, ROWS, PB), bf16),
            pltpu.VMEM((nb, ROWS, PB), bf16),
            pltpu.VMEM((NCOL, PB, 64), bf16),
            pltpu.VMEM((NCOL, PB, 48), bf16),
            pltpu.VMEM((NCOL, 3, PB, 128), f32),
            pltpu.VMEM((NCOL, 16, PB), f32),
            pltpu.VMEM((nb + 1, 4, 8, PB), f32),
            pltpu.VMEM((NROW, 8, 128), f32),
            pltpu.VMEM((NROW - 1, 8, 128), f32),
            pltpu.VMEM((8, 128), f32),
            pltpu.VMEM((NCOL - 1, 8, 128), f32),
            dma((6,)), dma((NCOL - 1,)), dma((NCOL - 1,)), dma((nb,)), dma((nb,)),
            dma((NROW - 1,)), dma((NROW - 1,)), dma((NCOL - 1,)), dma((NCOL - 1,)),
        ],
        compiler_params=pltpu.CompilerParams(
            collective_id=0, has_side_effects=True, vmem_limit_bytes=48 * 2**20
        ),
    )(positions, primal.T, adjoint.T, support, basis, sel)


def solution(mesh):
    in_specs = (
        P(None, ("row", "col")),
        P(("row", "col"), None),
        P(("row", "col"), None),
        P(None, ("row", "col")),
        P(None, ("row", "col")),
    )
    out_specs = P(None, ("row", "col"))
    return jax.shard_map(shards, mesh=mesh, in_specs=in_specs, out_specs=out_specs, check_vma=False)
```

time: 45.3 us -> 44.6 us (0.985)
  Pallas kernels: 42.7 us -> 39.2 us
  local copies, waits for them, and re-layouts: 2.33 us -> 4.96 us
    pallas_call x1, Pallas kernels: 42.7 us -> 39.2 us  [shards(): pl.pallas_call(kernel, out_shape=jax.ShapeDtypeStruct((3, 16), f32), in_s...]
    unnamed x13, local copies, waits for them, and re-layouts: 2.33 us -> 4.96 us
where the time goes in v2:
time: 44.6 us; the launch traced here: 44.2 us
  Pallas kernels  39.2 us (88%)
  local copies, waits for them, and re-layouts  4.96 us (11%)
    pallas_call x1, Pallas kernels, shards(): pl.pallas_call(kernel, out_shape=jax.ShapeDtypeStruct((3, 16), f32), in_s...  39.2 us
    unnamed x13, local copies, waits for them, and re-layouts  4.96 us

profile of v2, /device:TPU:1, one launch (start us, length us, event | category | flops | bytes accessed | tf_op | source)
XLA Modules:
  0.0 44.2 jit_solution(11367674452032367660)
XLA Ops:
  0.0 0.0 copy-start
  0.0 0.9 %copy-done = bf16[80,512]{1,0:T(8,128)(2,1)S(1)} copy-done((bf16[80,512]{1,0:T(8,128)(2,1)S(1)}, bf16[80,512]{1,0:T(8,128)(2,1)}, u32[]{:S(2)}) %copy-start) | copy-done | bytes 81944
  0.9 0.0 copy-start.1
  0.9 0.7 %copy-done.1 = bf16[256,32]{0,1:T(8,128)(2,1)S(1)} copy-done((bf16[256,32]{0,1:T(8,128)(2,1)S(1)}, bf16[256,32]{0,1:T(8,128)(2,1)}, u32[]{:S(2)}) %copy-start.1) | copy-done | bytes 16408
  1.6 0.0 copy-start.2
  1.6 0.7 %copy-done.2 = bf16[256,32]{0,1:T(8,128)(2,1)S(1)} copy-done((bf16[256,32]{0,1:T(8,128)(2,1)S(1)}, bf16[256,32]{0,1:T(8,128)(2,1)}, u32[]{:S(2)}) %copy-start.2) | copy-done | bytes 16408
  2.3 0.0 copy-start.3
  2.3 0.7 %copy-done.3 = f32[3,256]{1,0:T(4,128)S(1)} copy-done((f32[3,256]{1,0:T(4,128)S(1)}, f32[3,256]{1,0:T(4,128)}, u32[]{:S(2)}) %copy-start.3) | copy-done | bytes 3096
  3.0 0.0 copy-start.4
  3.0 0.7 %copy-done.4 = s32[4,256]{1,0:T(4,128)S(1)} copy-done((s32[4,256]{1,0:T(4,128)S(1)}, s32[4,256]{1,0:T(4,128)}, u32[]{:S(2)}) %copy-start.4) | copy-done | bytes 4120
  3.7 0.0 copy-start.5
  3.7 0.7 %copy-done.5 = f32[4,256]{1,0:T(4,128)S(1)} copy-done((f32[4,256]{1,0:T(4,128)S(1)}, f32[4,256]{1,0:T(4,128)}, u32[]{:S(2)}) %copy-start.5) | copy-done | bytes 4120
  4.4 39.2 %shard_map.64 = f32[3,16]{1,0:T(4,128)S(1)} custom-call(f32[3,256]{1,0:T(4,128)S(1)} %copy-done.3, bf16[32,256]{1,0:T(8,128)(2,1)S(1)} %bitcast.2, bf16[32,256]{1,0:T(8,128)(2,1)S(1)} %bitcast.3, s32[4,256]{1,0:T(4,128)S(1)} %copy-done.4, f32[4,256]{1,0:T(4,128)S(1)} %copy-done.5, bf16[80,512]{1,0:T(8,128)(2,1)S(1)} %copy-done), custom_call_target="tpu_custom_call" | custom-call | tf_op jit(solution)/shard_map/pallas_call | solution.py:289
  43.6 0.6 %copy.8 = f32[3,16]{1,0:T(4,128)} copy(f32[3,16]{1,0:T(4,128)S(1)} %shard_map.64) | data formatting | bytes 384
Async XLA Ops:
  0.0 0.9 %copy-start = (bf16[80,512]{1,0:T(8,128)(2,1)S(1)}, bf16[80,512]{1,0:T(8,128)(2,1)}, u32[]{:S(2)}) copy-start(bf16[80,512]{1,0:T(8,128)(2,1)} %constant.2.clone.sel_hbm) | copy-start | bytes 245764
  0.9 0.7 %copy-start.1 = (bf16[256,32]{0,1:T(8,128)(2,1)S(1)}, bf16[256,32]{0,1:T(8,128)(2,1)}, u32[]{:S(2)}) copy-start(bf16[256,32]{0,1:T(8,128)(2,1)} %param.7) | copy-start | bytes 49156
  1.6 0.7 %copy-start.2 = (bf16[256,32]{0,1:T(8,128)(2,1)S(1)}, bf16[256,32]{0,1:T(8,128)(2,1)}, u32[]{:S(2)}) copy-start(bf16[256,32]{0,1:T(8,128)(2,1)} %param.8) | copy-start | bytes 49156
  2.3 0.7 %copy-start.3 = (f32[3,256]{1,0:T(4,128)S(1)}, f32[3,256]{1,0:T(4,128)}, u32[]{:S(2)}) copy-start(f32[3,256]{1,0:T(4,128)} %pos_hbm.1) | copy-start | bytes 9220
  3.0 0.7 %copy-start.4 = (s32[4,256]{1,0:T(4,128)S(1)}, s32[4,256]{1,0:T(4,128)}, u32[]{:S(2)}) copy-start(s32[4,256]{1,0:T(4,128)} %sup_hbm.1) | copy-start | bytes 12292
  3.7 0.7 %copy-start.5 = (f32[4,256]{1,0:T(4,128)S(1)}, f32[4,256]{1,0:T(4,128)}, u32[]{:S(2)}) copy-start(f32[4,256]{1,0:T(4,128)} %bas_hbm.1) | copy-start | bytes 12292

commit v3 on v2

--- a/solution.py
+++ b/solution.py
@@ -1,4 +1,3 @@
-import numpy as np
 import jax
 import jax.numpy as jnp
 from jax import lax
@@ -17,28 +16,26 @@
 FULL = ((1, 0), (0, 1), (1, 1), (3, 1), (3, 2), (2, 3))
 HALF = ((2, 0), (0, 2), (2, 2))
 OFFS = FULL + HALF
+FAR = sorted(
+    ((x, y, z) for x in range(SIDE) for y in range(SIDE) for z in range(SIDE) if x or y or z),
+    key=lambda o: -sum(min(v, SIDE - v) for v in o),
+)
 ROWS = 96
 CHUNK = 32
 
 
 def selectors():
-    left = np.zeros((80, 512), np.float32)
-    for s in range(STR):
-        left[STR + s, s] = 1.0
-        left[s, STR + s] = 1.0
-    h, m, l, n, one = 64, 67, 70, 73, 76
-    for part, rows in enumerate((h, m, l)):
-        base = 64 + 16 * part
-        for c in range(3):
-            for slot in (c, 3 + c, 6 + c):
-                left[rows + c, base + slot] = -2.0
-        left[n + part, base + 12] = 1.0
-    for k in range(3):
-        left[one, 64 + 9 + k] = 1.0
-    for c in range(3):
-        for rows in (h, m, l):
-            left[rows + c, 128 + 128 * c : 256 + 128 * c] = 1.0
-    return left
+    r = lax.broadcasted_iota(jnp.int32, (80, 512), 0)
+    c = lax.broadcasted_iota(jnp.int32, (80, 512), 1)
+    weights = (c < 2 * STR) & (r < 2 * STR) & (r == (c + STR) % (2 * STR))
+    part, slot = (c - 64) // 16, c % 16
+    r3, slot3 = (r - 64) % 3, slot % 3
+    distance = (c >= 64) & (c < 112)
+    cross = distance & (slot < 9) & (r >= 64) & (r < 73) & ((r - 64) // 3 == part) & (r3 == slot3)
+    norm = distance & (slot == 12) & (r == 73 + part)
+    norm = norm | (distance & (part == 0) & (slot >= 9) & (slot < 12) & (r == 76))
+    spread = (c >= 128) & (r >= 64) & (r < 73) & (r3 == (c - 128) // 128)
+    return jnp.where(cross, -2.0, jnp.where(weights | norm | spread, 1.0, 0.0)).astype(bf16)
 
 
 def split3(x):
@@ -49,7 +46,7 @@
 
 
 def kernel(
-    pos_hbm, prim_hbm, adj_hbm, sup_hbm, bas_hbm, sel_hbm, out_ref,
+    pos_hbm, prim_hbm, adj_hbm, sup_hbm, bas_hbm, out_ref,
     pos_v, sup_v, bas_v, sel_v, ta, tb, aw, ad, xa, acc_a, acc_b, s1, r1, s2, r2,
     load, send_a, recv_a, send_b, recv_b, send_1, recv_1, send_2, recv_2,
 ):
@@ -72,13 +69,14 @@
     loads = [
         pltpu.make_async_copy(src, dst, load.at[i])
         for i, (src, dst) in enumerate((
-            (pos_hbm, pos_v), (sup_hbm, sup_v), (bas_hbm, bas_v), (sel_hbm, sel_v),
+            (pos_hbm, pos_v), (sup_hbm, sup_v), (bas_hbm, bas_v),
             (adj_hbm, ta.at[0, 0:32]), (prim_hbm, ta.at[0, 32:64]),
         ))
     ]
     for copy in loads:
         copy.start()
     acc_a[...] = jnp.zeros_like(acc_a)
+    sel_v[...] = selectors()
     for copy in loads[:3]:
         copy.wait()
     u = pos_v[...] - SHIFT
@@ -91,7 +89,8 @@
     sup = sup_v[...]
     bas = bas_v[...]
     bh = bas.astype(bf16).astype(f32)
-    feats += [(sup // 16).astype(f32), (sup % 16).astype(f32), bh, bas - bh]
+    point = sup // 16
+    feats += [((point % 2) * 64 + point // 2).astype(f32), (sup % 16).astype(f32), bh, bas - bh]
     ta[0, 64:96] = jnp.concatenate(feats, axis=0).astype(bf16)
     for copy in loads[3:]:
         copy.wait()
@@ -236,52 +235,45 @@
 
     total = jnp.zeros((128, 96), f32)
     total = scatter(total, from_a(0) + from_b(nb, own), own)
-    total = lax.fori_loop(1, NCOL, lambda d, t: scatter(t, from_a(d), ta.at[d]), total)
-    total = lax.fori_loop(0, nb, lambda k, t: scatter(t, from_b(k, tb.at[k]), tb.at[k]), total)
+    for slot in range(1, NCOL):
+        total = scatter(total, from_a(slot), ta.at[slot])
+    for k in range(nb):
+        total = scatter(total, from_b(k, tb.at[k]), tb.at[k])
     total = jnp.concatenate([total[:, 0:48] + total[:, 48:96], jnp.zeros((128, 80), f32)], axis=1)
 
-    s1[...] = total.reshape(NROW, NCOL, 128)
-
-    def copy_1(k):
-        other = at_row((k // SIDE, k % SIDE))
-        return pltpu.make_async_remote_copy(
-            src_ref=s1.at[other], dst_ref=r1.at[k - 1], send_sem=send_1.at[k - 1], recv_sem=recv_1.at[k - 1],
-            device_id=(other, col), device_id_type=MESH,
-        )
-
-    def copy_2(slot):
-        return pltpu.make_async_remote_copy(
-            src_ref=s2, dst_ref=r2.at[slot - 1], send_sem=send_2.at[slot - 1], recv_sem=recv_2.at[slot - 1],
-            device_id=(row, at_col(slot)), device_id_type=MESH,
-        )
-
-    for k in range(1, NROW):
-        copy_1(k).start()
-    mine = s1[row]
-    for k in range(1, NROW):
-        copy_1(k).wait_recv()
-        mine = mine + r1[k - 1]
-    s2[...] = mine
-    for slot in range(1, NCOL):
-        copy_2(slot).start()
-    for slot in range(1, NCOL):
-        copy_2(slot).wait_recv()
-        mine = mine + r2[slot - 1]
-    here = lax.broadcasted_iota(jnp.int32, (NCOL, 128), 0) == col
-    line = jnp.sum(jnp.where(here, mine, 0.0), axis=0, keepdims=True)
+    s1[...] = total.reshape(2, NROW * SIDE, 128)
+    sibling = pltpu.make_async_remote_copy(
+        src_ref=s1.at[1 - core], dst_ref=r1, send_sem=send_1, recv_sem=recv_1,
+        device_id=(row, at_col(1)), device_id_type=MESH,
+    )
+    sibling.start()
+    sibling.wait_recv()
+    both = s1[core] + r1[...]
+    for j in range(NROW * SIDE):
+        s2[j] = both[j : j + 1]
+    for j, (dx, dy, dz) in enumerate(FAR):
+        to_row, to_y = at_row((dx, dz)), (cy + dy) % SIDE
+        pltpu.make_async_remote_copy(
+            src_ref=s2.at[to_row * SIDE + to_y], dst_ref=r2.at[j], send_sem=send_2, recv_sem=recv_2,
+            device_id=(to_row, to_y * 2 + core), device_id_type=MESH,
+        ).start()
+    rows = pltpu.make_async_remote_copy(
+        src_ref=s2.at[0 : len(FAR)], dst_ref=r2, send_sem=send_2, recv_sem=recv_2,
+        device_id=(row, at_col(1)), device_id_type=MESH,
+    )
+    rows.wait_recv()
+    line = s2[row * SIDE + cy] + jnp.sum(r2[...], axis=0)
     out_ref[...] = jnp.concatenate([line[:, 16 * c : 16 * (c + 1)] for c in range(3)], axis=0)
 
     for slot in range(1, NCOL):
         copy_a(slot).wait_send()
-        copy_2(slot).wait_send()
     for k in range(nb):
         copy_b(k).wait_send()
-    for k in range(1, NROW):
-        copy_1(k).wait_send()
+    sibling.wait_send()
+    rows.wait_send()
 
 
 def shards(positions, primal, adjoint, support, basis):
-    sel = jnp.asarray(selectors(), bf16)
     vmem = pl.BlockSpec(memory_space=pltpu.VMEM)
     hbm = pl.BlockSpec(memory_space=pltpu.HBM)
     dma = pltpu.SemaphoreType.DMA
@@ -289,7 +281,7 @@
     return pl.pallas_call(
         kernel,
         out_shape=jax.ShapeDtypeStruct((3, 16), f32),
-        in_specs=[hbm] * 6,
+        in_specs=[hbm] * 5,
         out_specs=vmem,
         scratch_shapes=[
             pltpu.VMEM((3, PB), f32),
@@ -303,17 +295,17 @@
             pltpu.VMEM((NCOL, 3, PB, 128), f32),
             pltpu.VMEM((NCOL, 16, PB), f32),
             pltpu.VMEM((nb + 1, 4, 8, PB), f32),
-            pltpu.VMEM((NROW, 8, 128), f32),
-            pltpu.VMEM((NROW - 1, 8, 128), f32),
-            pltpu.VMEM((8, 128), f32),
-            pltpu.VMEM((NCOL - 1, 8, 128), f32),
-            dma((6,)), dma((NCOL - 1,)), dma((NCOL - 1,)), dma((nb,)), dma((nb,)),
-            dma((NROW - 1,)), dma((NROW - 1,)), dma((NCOL - 1,)), dma((NCOL - 1,)),
+            pltpu.VMEM((2, NROW * SIDE, 128), f32),
+            pltpu.VMEM((NROW * SIDE, 128), f32),
+            pltpu.VMEM((NROW * SIDE, 1, 128), f32),
+            pltpu.VMEM((NROW * SIDE - 1, 1, 128), f32),
+            dma((5,)), dma((NCOL - 1,)), dma((NCOL - 1,)), dma((nb,)), dma((nb,)),
+            dma, dma, dma, dma,
         ],
         compiler_params=pltpu.CompilerParams(
-            collective_id=0, has_side_effects=True, vmem_limit_bytes=48 * 2**20
+            collective_id=0, has_side_effects=True, vmem_limit_bytes=60 * 2**20
         ),
-    )(positions, primal.T, adjoint.T, support, basis, sel)
+    )(positions, primal.T, adjoint.T, support, basis)
 
 
 def solution(mesh):

time: 44.6 us -> 36.1 us (0.81)
  Pallas kernels: 39.2 us -> 34.7 us
  local copies, waits for them, and re-layouts: 4.96 us -> 1.26 us
    pallas_call x1, Pallas kernels: 39.2 us -> 34.7 us  [shards(): pl.pallas_call(kernel, out_shape=jax.ShapeDtypeStruct((3, 16), f32), in_s...]
    unnamed x13 -> x1, local copies, waits for them, and re-layouts: 4.96 us -> 1.26 us
where the time goes in v3:
time: 36.1 us; the launch traced here: 35.9 us
  Pallas kernels  34.7 us (96%)
  local copies, waits for them, and re-layouts  1.26 us (3%)
    pallas_call x1, Pallas kernels, shards(): pl.pallas_call(kernel, out_shape=jax.ShapeDtypeStruct((3, 16), f32), in_s...  34.7 us
    unnamed x1, local copies, waits for them, and re-layouts  1.26 us

profile of v3, /device:TPU:1, one launch (start us, length us, event | category | flops | bytes accessed | tf_op | source)
XLA Modules:
  0.0 35.9 jit_solution(5599051721877341250)
XLA Ops:
  0.0 34.7 %shard_map.55 = f32[3,16]{1,0:T(4,128)} custom-call(f32[3,256]{1,0:T(4,128)} %pos_hbm.1, bf16[32,256]{1,0:T(8,128)(2,1)} %bitcast.2, bf16[32,256]{1,0:T(8,128)(2,1)} %bitcast.3, s32[4,256]{1,0:T(4,128)} %sup_hbm.1, f32[4,256]{1,0:T(4,128)} %bas_hbm.1), custom_call_target="tpu_custom_call" | custom-call | tf_op jit(solution)/shard_map/pallas_call | solution.py:281
  34.7 1.3 %copy.7 = f32[3,16]{1,0:T(4,128)} copy(f32[3,16]{1,0:T(4,128)} %shard_map.55) | data formatting | bytes 384

commit v4 on v3

--- a/solution.py
+++ b/solution.py
@@ -98,11 +98,18 @@
     pl.semaphore_wait(barrier, NCOL - 1 + NROW - 1)
 
     def copy_a(slot):
-        src = 0 if slot % 2 == 0 or slot == 1 else slot - 1
+        src = 0 if slot in (1, 2, 6) else slot - 1
         to = at_col(slot, -1) if src == 0 else at_col(1)
         return pltpu.make_async_remote_copy(
             src_ref=ta.at[src], dst_ref=ta.at[slot], send_sem=send_a.at[slot - 1], recv_sem=recv_a.at[slot - 1],
             device_id=(row, to), device_id_type=MESH,
+        )
+
+    def pass_on(slot):
+        half, sem = (slice(0, ROWS // 2), 3) if slot == 2 else (slice(ROWS // 2, ROWS), 7)
+        return pltpu.make_async_remote_copy(
+            src_ref=ta.at[slot, half], dst_ref=ta.at[4, half], send_sem=send_a.at[sem], recv_sem=recv_a.at[sem],
+            device_id=(row, at_col(slot, -1)), device_id_type=MESH,
         )
 
     def copy_b(k):
@@ -112,7 +119,7 @@
             device_id=(at_row((-off[0], -off[1])), col), device_id_type=MESH,
         )
 
-    for slot in (1, 2, 6, 4):
+    for slot in (1, 2, 6):
         copy_a(slot).start()
     for k in (0, 1):
         copy_b(k).start()
@@ -164,27 +171,47 @@
     copy_a(1).wait_recv()
     prepare(1)
     pairs(own, [1], nb, half=(0,), first=False)
-    for slot in (2, 6, 4):
-        copy_a(slot).wait_recv()
-        copy_a(slot + 1).start()
-    for k in (2, 3, 4):
-        copy_b(k).start()
-    prepare(2)
-    prepare(4)
-    prepare(6)
-    pairs(own, [2, 4], nb, half=(1,), first=False)
-    for k in range(5, nb):
-        copy_b(k).start()
-    for slot in (3, 7, 5):
-        copy_a(slot).wait_recv()
-        prepare(slot)
-    pairs(own, [3, 5], nb, half=(1,), first=False)
-
     def arrived(k):
         pltpu.make_async_remote_copy(
             src_ref=ta.at[0], dst_ref=tb.at[k], send_sem=send_b.at[k], recv_sem=recv_b.at[k],
             device_id=(row, at_col(1)), device_id_type=MESH,
         ).wait_recv()
+
+    def early(slots, first):
+        def body(k, _):
+            if first:
+                arrived(k)
+            pairs(tb.at[k], slots, k, first=first)
+            return 0
+
+        lax.fori_loop(0, 2, body, 0)
+
+    for slot in (2, 6):
+        copy_a(slot).wait_recv()
+        pass_on(slot).start()
+        copy_a(slot + 1).start()
+    for k in (2, 3):
+        copy_b(k).start()
+    prepare(2)
+    prepare(6)
+    pairs(own, [2], nb, first=False)
+    early([0, 1, 2, 6], True)
+    for k in range(4, nb):
+        copy_b(k).start()
+    for slot in (3, 7):
+        copy_a(slot).wait_recv()
+        prepare(slot)
+    pairs(own, [3], nb, first=False)
+    early([3, 7], False)
+    pass_on(2).wait_recv()
+    pass_on(6).wait_recv()
+    copy_a(5).start()
+    prepare(4)
+    pairs(own, [4], nb, half=(0,), first=False)
+    copy_a(5).wait_recv()
+    prepare(5)
+    pairs(own, [5], nb, half=(0,), first=False)
+    early([4, 5], False)
 
     def full(k, _):
         arrived(k)
@@ -198,7 +225,7 @@
         pairs(tb.at[k], [first + j for j in range(4)], k)
         return 0
 
-    lax.fori_loop(0, len(FULL), full, 0)
+    lax.fori_loop(2, len(FULL), full, 0)
     lax.fori_loop(len(FULL), nb, halved, 0)
 
     def coords(bundle):
@@ -265,8 +292,10 @@
     line = s2[row * SIDE + cy] + jnp.sum(r2[...], axis=0)
     out_ref[...] = jnp.concatenate([line[:, 16 * c : 16 * (c + 1)] for c in range(3)], axis=0)
 
-    for slot in range(1, NCOL):
+    for slot in (1, 2, 3, 5, 6, 7):
         copy_a(slot).wait_send()
+    pass_on(2).wait_send()
+    pass_on(6).wait_send()
     for k in range(nb):
         copy_b(k).wait_send()
     sibling.wait_send()
@@ -299,11 +328,11 @@
             pltpu.VMEM((NROW * SIDE, 128), f32),
             pltpu.VMEM((NROW * SIDE, 1, 128), f32),
             pltpu.VMEM((NROW * SIDE - 1, 1, 128), f32),
-            dma((5,)), dma((NCOL - 1,)), dma((NCOL - 1,)), dma((nb,)), dma((nb,)),
+            dma((5,)), dma((NCOL,)), dma((NCOL,)), dma((nb,)), dma((nb,)),
             dma, dma, dma, dma,
         ],
         compiler_params=pltpu.CompilerParams(
-            collective_id=0, has_side_effects=True, vmem_limit_bytes=60 * 2**20
+            collective_id=0, has_side_effects=True, vmem_limit_bytes=55227 * 2**10
         ),
     )(positions, primal.T, adjoint.T, support, basis)
 

time: 36.1 us -> 34.9 us (0.967)
  local copies, waits for them, and re-layouts: 1.26 us -> 0.58 us
  Pallas kernels: 34.7 us -> 34.2 us
    unnamed x1, local copies, waits for them, and re-layouts: 1.26 us -> 0.58 us
    pallas_call x1, Pallas kernels: 34.7 us -> 34.2 us  [shards(): pl.pallas_call(kernel, out_shape=jax.ShapeDtypeStruct((3, 16), f32), in_s...]
where the time goes in v4:
time: 34.9 us; the launch traced here: 34.8 us
  Pallas kernels  34.2 us (98%)
  local copies, waits for them, and re-layouts  0.58 us (2%)
    pallas_call x1, Pallas kernels, shards(): pl.pallas_call(kernel, out_shape=jax.ShapeDtypeStruct((3, 16), f32), in_s...  34.2 us

profile of v4, /device:TPU:1, one launch (start us, length us, event | category | flops | bytes accessed | tf_op | source)
XLA Modules:
  0.0 34.8 jit_solution(3325378914003664521)
XLA Ops:
  0.0 34.2 %shard_map.55 = f32[3,16]{1,0:T(4,128)S(1)} custom-call(f32[3,256]{1,0:T(4,128)} %pos_hbm.1, bf16[32,256]{1,0:T(8,128)(2,1)} %bitcast.2, bf16[32,256]{1,0:T(8,128)(2,1)} %bitcast.3, s32[4,256]{1,0:T(4,128)} %sup_hbm.1, f32[4,256]{1,0:T(4,128)} %bas_hbm.1), custom_call_target="tpu_custom_call" | custom-call | tf_op jit(solution)/shard_map/pallas_call | solution.py:310
  34.2 0.6 %copy.7 = f32[3,16]{1,0:T(4,128)} copy(f32[3,16]{1,0:T(4,128)S(1)} %shard_map.55) | data formatting | bytes 384

commit v5 on v4

--- a/solution.py
+++ b/solution.py
@@ -1,3 +1,4 @@
+import numpy as np
 import jax
 import jax.numpy as jnp
 from jax import lax
@@ -17,8 +18,8 @@
 HALF = ((2, 0), (0, 2), (2, 2))
 OFFS = FULL + HALF
 FAR = sorted(
-    ((x, y, z) for x in range(SIDE) for y in range(SIDE) for z in range(SIDE) if x or y or z),
-    key=lambda o: -sum(min(v, SIDE - v) for v in o),
+    (o for o in np.ndindex(SIDE, SIDE, SIDE, 2) if any(o)),
+    key=lambda o: -sum(min(v, SIDE - v) for v in o[:3]) - 0.5 * o[3],
 )
 ROWS = 96
 CHUNK = 32
@@ -47,8 +48,8 @@
 
 def kernel(
     pos_hbm, prim_hbm, adj_hbm, sup_hbm, bas_hbm, out_ref,
-    pos_v, sup_v, bas_v, sel_v, ta, tb, aw, ad, xa, acc_a, acc_b, s1, r1, s2, r2,
-    load, send_a, recv_a, send_b, recv_b, send_1, recv_1, send_2, recv_2,
+    pos_v, sup_v, bas_v, sel_v, ta, tb, aw, ad, xa, acc_a, acc_b, s1, r1,
+    load, send_a, recv_a, send_b, recv_b, send_1, recv_1,
 ):
     row, col = lax.axis_index("row"), lax.axis_index("col")
     rx, rz, cy, core = row // SIDE, row % SIDE, col // 2, col % 2
@@ -200,18 +201,15 @@
         copy_b(k).start()
     for slot in (3, 7):
         copy_a(slot).wait_recv()
-        prepare(slot)
-    pairs(own, [3], nb, first=False)
-    early([3, 7], False)
     pass_on(2).wait_recv()
     pass_on(6).wait_recv()
     copy_a(5).start()
-    prepare(4)
-    pairs(own, [4], nb, half=(0,), first=False)
+    for slot in (3, 7, 4):
+        prepare(slot)
     copy_a(5).wait_recv()
     prepare(5)
-    pairs(own, [5], nb, half=(0,), first=False)
-    early([4, 5], False)
+    pairs(own, [3, 4, 5], nb, half=(1, 2), first=False)
+    early([3, 7, 4, 5], False)
 
     def full(k, _):
         arrived(k)
@@ -268,28 +266,24 @@
         total = scatter(total, from_b(k, tb.at[k]), tb.at[k])
     total = jnp.concatenate([total[:, 0:48] + total[:, 48:96], jnp.zeros((128, 80), f32)], axis=1)
 
-    s1[...] = total.reshape(2, NROW * SIDE, 128)
-    sibling = pltpu.make_async_remote_copy(
-        src_ref=s1.at[1 - core], dst_ref=r1, send_sem=send_1, recv_sem=recv_1,
-        device_id=(row, at_col(1)), device_id_type=MESH,
-    )
-    sibling.start()
-    sibling.wait_recv()
-    both = s1[core] + r1[...]
-    for j in range(NROW * SIDE):
-        s2[j] = both[j : j + 1]
-    for j, (dx, dy, dz) in enumerate(FAR):
-        to_row, to_y = at_row((dx, dz)), (cy + dy) % SIDE
+    for j in range(NROW * NCOL):
+        s1[j] = total[j : j + 1]
+
+    def row_of(to_row, to_y, to_core):
+        return (to_core * NROW + to_row) * SIDE + to_y
+
+    for j, (dx, dy, dz, dc) in enumerate(FAR):
+        to_row, to_y, to_core = at_row((dx, dz)), (cy + dy) % SIDE, (core + dc) % 2
         pltpu.make_async_remote_copy(
-            src_ref=s2.at[to_row * SIDE + to_y], dst_ref=r2.at[j], send_sem=send_2, recv_sem=recv_2,
-            device_id=(to_row, to_y * 2 + core), device_id_type=MESH,
+            src_ref=s1.at[row_of(to_row, to_y, to_core)], dst_ref=r1.at[j], send_sem=send_1, recv_sem=recv_1,
+            device_id=(to_row, to_y * 2 + to_core), device_id_type=MESH,
         ).start()
     rows = pltpu.make_async_remote_copy(
-        src_ref=s2.at[0 : len(FAR)], dst_ref=r2, send_sem=send_2, recv_sem=recv_2,
+        src_ref=s1.at[0 : len(FAR)], dst_ref=r1, send_sem=send_1, recv_sem=recv_1,
         device_id=(row, at_col(1)), device_id_type=MESH,
     )
     rows.wait_recv()
-    line = s2[row * SIDE + cy] + jnp.sum(r2[...], axis=0)
+    line = s1[row_of(row, cy, core)] + jnp.sum(r1[...], axis=0)
     out_ref[...] = jnp.concatenate([line[:, 16 * c : 16 * (c + 1)] for c in range(3)], axis=0)
 
     for slot in (1, 2, 3, 5, 6, 7):
@@ -298,7 +292,6 @@
     pass_on(6).wait_send()
     for k in range(nb):
         copy_b(k).wait_send()
-    sibling.wait_send()
     rows.wait_send()
 
 
@@ -324,12 +317,10 @@
             pltpu.VMEM((NCOL, 3, PB, 128), f32),
             pltpu.VMEM((NCOL, 16, PB), f32),
             pltpu.VMEM((nb + 1, 4, 8, PB), f32),
-            pltpu.VMEM((2, NROW * SIDE, 128), f32),
-            pltpu.VMEM((NROW * SIDE, 128), f32),
-            pltpu.VMEM((NROW * SIDE, 1, 128), f32),
-            pltpu.VMEM((NROW * SIDE - 1, 1, 128), f32),
+            pltpu.VMEM((NROW * NCOL, 1, 128), f32),
+            pltpu.VMEM((NROW * NCOL - 1, 1, 128), f32),
             dma((5,)), dma((NCOL,)), dma((NCOL,)), dma((nb,)), dma((nb,)),
-            dma, dma, dma, dma,
+            dma, dma,
         ],
         compiler_params=pltpu.CompilerParams(
             collective_id=0, has_side_effects=True, vmem_limit_bytes=55227 * 2**10

time: 34.9 us -> 34.1 us (0.977)
  Pallas kernels: 34.2 us -> 33.4 us
    pallas_call x1, Pallas kernels: 34.2 us -> 33.4 us  [shards(): pl.pallas_call(kernel, out_shape=jax.ShapeDtypeStruct((3, 16), f32), in_s...]
where the time goes in v5:
time: 34.1 us; the launch traced here: 34 us
  Pallas kernels  33.4 us (98%)
  local copies, waits for them, and re-layouts  0.58 us (2%)
    pallas_call x1, Pallas kernels, shards(): pl.pallas_call(kernel, out_shape=jax.ShapeDtypeStruct((3, 16), f32), in_s...  33.4 us

profile of v5, /device:TPU:1, one launch (start us, length us, event | category | flops | bytes accessed | tf_op | source)
XLA Modules:
  0.0 34.0 jit_solution(1962870870356229986)
XLA Ops:
  0.0 33.4 %shard_map.55 = f32[3,16]{1,0:T(4,128)S(1)} custom-call(f32[3,256]{1,0:T(4,128)} %pos_hbm.1, bf16[32,256]{1,0:T(8,128)(2,1)} %bitcast.2, bf16[32,256]{1,0:T(8,128)(2,1)} %bitcast.3, s32[4,256]{1,0:T(4,128)} %sup_hbm.1, f32[4,256]{1,0:T(4,128)} %bas_hbm.1), custom_call_target="tpu_custom_call" | custom-call | tf_op jit(solution)/shard_map/pallas_call | solution.py:303
  33.4 0.6 %copy.7 = f32[3,16]{1,0:T(4,128)} copy(f32[3,16]{1,0:T(4,128)S(1)} %shard_map.55) | data formatting | bytes 384

commit v6 on v5

--- a/solution.py
+++ b/solution.py
@@ -212,8 +212,10 @@
     early([3, 7, 4, 5], False)
 
     def full(k, _):
-        arrived(k)
-        pairs(tb.at[k], range(NCOL), k)
+        for j in range(2):
+            arrived(2 * k + j)
+        for j in range(2):
+            pairs(tb.at[2 * k + j], range(NCOL), 2 * k + j)
         return 0
 
     def halved(k, _):
@@ -223,7 +225,7 @@
         pairs(tb.at[k], [first + j for j in range(4)], k)
         return 0
 
-    lax.fori_loop(2, len(FULL), full, 0)
+    lax.fori_loop(1, len(FULL) // 2, full, 0)
     lax.fori_loop(len(FULL), nb, halved, 0)
 
     def coords(bundle):
@@ -266,8 +268,7 @@
         total = scatter(total, from_b(k, tb.at[k]), tb.at[k])
     total = jnp.concatenate([total[:, 0:48] + total[:, 48:96], jnp.zeros((128, 80), f32)], axis=1)
 
-    for j in range(NROW * NCOL):
-        s1[j] = total[j : j + 1]
+    s1[...] = total.reshape(NROW * NCOL, 1, 128)
 
     def row_of(to_row, to_y, to_core):
         return (to_core * NROW + to_row) * SIDE + to_y

time: 34.1 us -> 33.9 us (level)
  no operation moved by 1% of the time
where the time goes in v6:
time: 33.9 us; the launch traced here: 33.7 us
  Pallas kernels  33.1 us (98%)
  local copies, waits for them, and re-layouts  0.58 us (2%)
    pallas_call x1, Pallas kernels, shards(): pl.pallas_call(kernel, out_shape=jax.ShapeDtypeStruct((3, 16), f32), in_s...  33.1 us

profile of v6, /device:TPU:1, one launch (start us, length us, event | category | flops | bytes accessed | tf_op | source)
XLA Modules:
  0.0 33.7 jit_solution(1042908458948369326)
XLA Ops:
  0.0 33.1 %shard_map.55 = f32[3,16]{1,0:T(4,128)S(1)} custom-call(f32[3,256]{1,0:T(4,128)} %pos_hbm.1, bf16[32,256]{1,0:T(8,128)(2,1)} %bitcast.2, bf16[32,256]{1,0:T(8,128)(2,1)} %bitcast.3, s32[4,256]{1,0:T(4,128)} %sup_hbm.1, f32[4,256]{1,0:T(4,128)} %bas_hbm.1), custom_call_target="tpu_custom_call" | custom-call | tf_op jit(solution)/shard_map/pallas_call | solution.py:304
  33.1 0.6 %copy.7 = f32[3,16]{1,0:T(4,128)} copy(f32[3,16]{1,0:T(4,128)S(1)} %shard_map.55) | data formatting | bytes 384

commit v7 on v6

--- a/solution.py
+++ b/solution.py
@@ -60,13 +60,6 @@
     def at_col(slot, sign=1):
         return ((cy + sign * (slot // 2)) % SIDE) * 2 + (core + slot) % 2
 
-    barrier = pltpu.get_barrier_semaphore()
-    for slot in range(1, NCOL):
-        pl.semaphore_signal(barrier, inc=1, device_id=(row, at_col(slot)), device_id_type=MESH)
-    for k in range(1, NROW):
-        other = at_row((k // SIDE, k % SIDE))
-        pl.semaphore_signal(barrier, inc=1, device_id=(other, col), device_id_type=MESH)
-
     loads = [
         pltpu.make_async_copy(src, dst, load.at[i])
         for i, (src, dst) in enumerate((
@@ -76,6 +69,13 @@
     ]
     for copy in loads:
         copy.start()
+    barrier = pltpu.get_barrier_semaphore()
+    for slot in range(1, NCOL):
+        pl.semaphore_signal(barrier, inc=1, device_id=(row, at_col(slot)), device_id_type=MESH)
+    for k in sorted(range(1, NROW), key=lambda k: sum(min(v, SIDE - v) for v in divmod(k, SIDE))):
+        other = at_row((k // SIDE, k % SIDE))
+        pl.semaphore_signal(barrier, inc=1, device_id=(other, col), device_id_type=MESH)
+
     acc_a[...] = jnp.zeros_like(acc_a)
     sel_v[...] = selectors()
     for copy in loads[:3]:
@@ -195,7 +195,6 @@
         copy_b(k).start()
     prepare(2)
     prepare(6)
-    pairs(own, [2], nb, first=False)
     early([0, 1, 2, 6], True)
     for k in range(4, nb):
         copy_b(k).start()
@@ -208,7 +207,7 @@
         prepare(slot)
     copy_a(5).wait_recv()
     prepare(5)
-    pairs(own, [3, 4, 5], nb, half=(1, 2), first=False)
+    pairs(own, [2, 3, 4, 5], nb, half=(2, 3), first=False)
     early([3, 7, 4, 5], False)
 
     def full(k, _):

time: 33.9 us -> 33.9 us (level)
  no operation moved by 1% of the time
where the time goes in v7:
time: 33.9 us; the launch traced here: 33.7 us
  Pallas kernels  33.1 us (98%)
  local copies, waits for them, and re-layouts  0.58 us (2%)
    pallas_call x1, Pallas kernels, shards(): pl.pallas_call(kernel, out_shape=jax.ShapeDtypeStruct((3, 16), f32), in_s...  33.1 us

profile of v7, /device:TPU:1, one launch (start us, length us, event | category | flops | bytes accessed | tf_op | source)
XLA Modules:
  0.0 33.7 jit_solution(14487486322952404592)
XLA Ops:
  0.0 33.1 %shard_map.55 = f32[3,16]{1,0:T(4,128)S(1)} custom-call(f32[3,256]{1,0:T(4,128)} %pos_hbm.1, bf16[32,256]{1,0:T(8,128)(2,1)} %bitcast.2, bf16[32,256]{1,0:T(8,128)(2,1)} %bitcast.3, s32[4,256]{1,0:T(4,128)} %sup_hbm.1, f32[4,256]{1,0:T(4,128)} %bas_hbm.1), custom_call_target="tpu_custom_call" | custom-call | tf_op jit(solution)/shard_map/pallas_call | solution.py:303
  33.1 0.6 %copy.7 = f32[3,16]{1,0:T(4,128)} copy(f32[3,16]{1,0:T(4,128)S(1)} %shard_map.55) | data formatting | bytes 384

commit v8 on v7

--- a/solution.py
+++ b/solution.py
@@ -272,8 +272,10 @@
     def row_of(to_row, to_y, to_core):
         return (to_core * NROW + to_row) * SIDE + to_y
 
+    xs, ys, zs = ([(p + d) % SIDE for d in range(SIDE)] for p in (rx, cy, rz))
+    cores = [core, 1 - core]
     for j, (dx, dy, dz, dc) in enumerate(FAR):
-        to_row, to_y, to_core = at_row((dx, dz)), (cy + dy) % SIDE, (core + dc) % 2
+        to_row, to_y, to_core = xs[dx] * SIDE + zs[dz], ys[dy], cores[dc]
         pltpu.make_async_remote_copy(
             src_ref=s1.at[row_of(to_row, to_y, to_core)], dst_ref=r1.at[j], send_sem=send_1, recv_sem=recv_1,
             device_id=(to_row, to_y * 2 + to_core), device_id_type=MESH,

time: 33.9 us -> 33.9 us (level)
  no operation moved by 1% of the time
where the time goes in v8:
time: 33.9 us; the launch traced here: 33.7 us
  Pallas kernels  33.1 us (98%)
  local copies, waits for them, and re-layouts  0.58 us (2%)
    pallas_call x1, Pallas kernels, shards(): pl.pallas_call(kernel, out_shape=jax.ShapeDtypeStruct((3, 16), f32), in_s...  33.1 us

profile of v8, /device:TPU:1, one launch (start us, length us, event | category | flops | bytes accessed | tf_op | source)
XLA Modules:
  0.0 33.7 jit_solution(13530569635356103710)
XLA Ops:
  0.0 33.1 %shard_map.55 = f32[3,16]{1,0:T(4,128)S(1)} custom-call(f32[3,256]{1,0:T(4,128)} %pos_hbm.1, bf16[32,256]{1,0:T(8,128)(2,1)} %bitcast.2, bf16[32,256]{1,0:T(8,128)(2,1)} %bitcast.3, s32[4,256]{1,0:T(4,128)} %sup_hbm.1, f32[4,256]{1,0:T(4,128)} %bas_hbm.1), custom_call_target="tpu_custom_call" | custom-call | tf_op jit(solution)/shard_map/pallas_call | solution.py:305
  33.1 0.6 %copy.7 = f32[3,16]{1,0:T(4,128)} copy(f32[3,16]{1,0:T(4,128)S(1)} %shard_map.55) | data formatting | bytes 384
